TPU v7x, 32 devices: a whole 2x2x4 slice. The times are simulated.
32 devices in a mesh: chan: 4 (over z), space: 8 (over y, x, core).
Axes of the slice: x: 2, y: 2, z: 4, core: 2. Of those that a mesh axis runs over, the one named last changes fastest.
Arguments:
- blocks: bfloat16 [512, 8192], P('space', 'chan'), may hold values from -10 to 10
- weight_one: bfloat16 [9, 512, 512], P(None, 'chan'), may hold values from -0.09375 to 0.09375
- weight_two: bfloat16 [9, 512, 512], P(None, 'chan'), may hold values from -0.09375 to 0.09375
- gain_one: float32 [512], P('chan'), may hold values from 0.5 to 1.5
- shift_one: float32 [512], P('chan'), may hold values from -3 to 3
- gain_two: float32 [512], P('chan'), may hold values from 0.5 to 1.5
- shift_two: float32 [512], P('chan'), may hold values from -3 to 3
- cell_live: int32 [512, 16], P('space'), may hold values from 0 to 1, as said below
- cotangent: bfloat16 [512, 8192], P('space', 'chan'), may hold values from -6 to 6
Outputs:
- block_out: bfloat16 [512, 8192], P('space', 'chan')
- input_grad: float32 [512, 8192], P('space', 'chan')
- weight_one_grad: float32 [9, 512, 512], P(None, 'chan')
- weight_two_grad: float32 [9, 512, 512], P(None, 'chan')
- gain_one_grad: float32 [512], P('chan')
- shift_one_grad: float32 [512], P('chan')
- gain_two_grad: float32 [512], P('chan')
- shift_two_grad: float32 [512], P('chan')
Inputs may be any that keep to these rules, and one draw needn't show every extreme that they name: `cell_live`: 1 marks a pixel of an image, 0 an empty cell; images are 7 x 7 or 3 x 3 crops (cut at the strip's two ends), and any two images are parted by empty rows and columns.
All inputs are finite; a program needn't handle non-finite values.
Results may differ from a plain program's by a relative error of at most 0.0059.
Values may be sent and summed in bfloat16 or wider, within the bound.
A program may use at most 128 MiB of HBM per device.

v0:
```python
import functools
import math

import jax
import jax.numpy as jnp
from jax import lax
from jax.experimental import pallas as pl
from jax.experimental.pallas import tpu as pltpu
from jax.sharding import PartitionSpec as P

EPSILON = 1e-05
MESH = pl.DeviceIdType.MESH
F32 = jnp.float32
BF16 = jnp.bfloat16
ROOT_HALF = 0.7071067811865476
ROOT_TWO_PI = 0.3989422804014327
CHUNK = 64
FINISH_PARTS = 4
UNROLL = 2
HALVES = 2
LARGE, SMALL = 7, 3


def dot(a, b):
    return jnp.dot(a, b, preferred_element_type=F32)


def gelu_parts(v):
    upper = 0.5 * (1.0 + lax.erf(v * ROOT_HALF))
    slope = upper + v * (ROOT_TWO_PI * jnp.exp(-0.5 * v * v))
    return v * upper, slope


def most_live(rows, wide):
    units = (wide + 1) // (SMALL + 1)
    live_rows = rows - rows // (LARGE + 1)
    return min(rows * wide, math.ceil(units * live_rows * LARGE / 2))


def block_kernel(n, s_count, rows, wide, ch, aligned, packed, *refs):
    (x_in, cot_in, live_in, gain1_in, shift1_in, gain2_in, shift2_in, w1_hbm, w2_hbm) = refs[:9]
    (out_block, out_input, out_wg1, out_wg2, out_gain1, out_shift1, out_gain2, out_shift2) = refs[9:17]
    (turned, wv, wf, x_t, pack, unpack, places, edge_send, edge_recv, cot_send, cot_recv, cotm, mask, masked,
     normed1, normed2, through, slope1, hid, hid2, pad, acc, hold, taken,
     part, psend, crecv, hsend, qrecv, wout, st_send, st_recv, row_send, row_recv,
     w_sem, wz_ssem, wz_rsem, wp_ssem, wp_rsem, e_ssem, e_rsem, ce_ssem, ce_rsem, ag_ssem, ag_rsem,
     st_ssem, st_rsem, row_ssem, row_rsem, c_ssem, c_rsem, q_ssem, q_rsem,
     f_ssem, f_rsem, h_ssem, h_rsem, o_sem) = refs[17:]

    z = lax.axis_index("chan")
    s = lax.axis_index("space")
    cells = rows * wide
    total = cells + 2 * wide
    band = cells // HALVES
    core, chip, chips = s % 2, s // 2, s_count // 2
    before, after = (s + s_count - 1) % s_count, (s + 1) % s_count
    tap_rows = 9 * ch

    barrier = pltpu.get_barrier_semaphore()

    @pl.loop(1, s_count)
    def _(k):
        pl.semaphore_signal(barrier, inc=1, device_id=(z, (s + k) % s_count), device_id_type=MESH)

    @pl.loop(1, n)
    def _(k):
        pl.semaphore_signal(barrier, inc=1, device_id=((z + k) % n, s), device_id_type=MESH)

    w_copies = []
    for which, source in enumerate((w1_hbm, w2_hbm)):
        for d in range(n):
            block = source.at[:, d * ch:(d + 1) * ch] if aligned else source.at[d]
            w_copies.append(pltpu.make_async_copy(block, wv.at[which, d], w_sem.at[which, d]))
    for copy in w_copies:
        copy.start()

    def chunked(fn, init, first=0, count=cells):
        def step(i, carry):
            return fn(pl.multiple_of(first + i * CHUNK, CHUNK), CHUNK, carry)
        return lax.fori_loop(0, count // CHUNK, step, init, unroll=UNROLL)

    lanes = 128
    tiles = ch * wide // lanes

    def from_flat(flat, put):
        for i in range(tiles):
            turned[i * lanes:(i + 1) * lanes, 0:rows] = flat[:, i * lanes:(i + 1) * lanes].astype(F32).T
        for w in range(wide):
            put(pl.ds(w, rows, stride=wide), turned[pl.ds(w, ch, stride=wide), 0:rows].T)

    def to_flat(source, flat):
        for w in range(wide):
            turned[pl.ds(w, ch, stride=wide), 0:rows] = source[pl.ds(w, rows, stride=wide), :].T
        for i in range(tiles):
            flat[:, i * lanes:(i + 1) * lanes] = turned[i * lanes:(i + 1) * lanes, 0:rows].T.astype(flat.dtype)

    def put_masked(at, value):
        masked[at, :] = value

    from_flat(x_in, put_masked)

    cell = lax.broadcasted_iota(jnp.int32, (cells, rows), 0)
    pick = (cell // wide == lax.broadcasted_iota(jnp.int32, (cells, rows), 1)).astype(F32).astype(BF16)
    column_of = lax.broadcasted_iota(jnp.int32, (cells, wide), 0) % wide
    picked = lax.dot_general(pick, live_in[...].astype(BF16), (((1,), (1,)), ((), ())), preferred_element_type=F32)
    picked = jnp.where(column_of == lax.broadcasted_iota(jnp.int32, (cells, wide), 1), picked, 0.0)
    mask[0:cells, :] = dot(picked.astype(BF16), jnp.ones((wide, ch), BF16))

    def load_main(start, size, carry):
        at = pl.ds(start, size)
        lv = mask[at, :]
        masked[at, :] = masked[at, :] * lv
        return carry

    chunked(load_main, 0)
    for side, start in ((0, 0), (1, cells - wide)):
        edge_send[side, 0] = masked[start:start + wide, :].astype(BF16)
        edge_send[side, 1] = mask[start:start + wide, :].astype(BF16)

    acc[...] = jnp.zeros_like(acc)
    for block in range(n):
        for row in (rows // HALVES + 1, rows + 2):
            taken[block, row:row + 1, :, :] = jnp.zeros((1, wide, 3 * ch), BF16)
    st_send[...] = jnp.zeros_like(st_send)

    pl.semaphore_wait(barrier, s_count - 1 + n - 1)

    def edge_copy(side):
        return pltpu.make_async_remote_copy(
            src_ref=edge_send.at[side], dst_ref=edge_recv.at[1 - side],
            send_sem=e_ssem.at[side], recv_sem=e_rsem.at[1 - side],
            device_id=(z, before if side == 0 else after), device_id_type=MESH)

    for side in range(2):
        edge_copy(side).start()

    def cot_copy(side):
        return pltpu.make_async_remote_copy(
            src_ref=cot_send.at[side], dst_ref=cot_recv.at[1 - side],
            send_sem=ce_ssem.at[side], recv_sem=ce_rsem.at[1 - side],
            device_id=(z, before if side == 0 else after), device_id_type=MESH)

    def load_cotangent():
        def put(at, value):
            cotm[at, :] = value
        from_flat(cot_in, put)

        def live_only(start, size, carry):
            at = pl.ds(start, size)
            cotm[at, :] = cotm[at, :] * mask[at, :]
            return carry
        chunked(live_only, 0)
        for side, start in ((0, 0), (1, cells - wide)):
            cot_send[side] = cotm[start:start + wide, :].astype(BF16)
            cot_copy(side).start()

    def take_cotangent():
        for side in range(2):
            cot_copy(1 - side).wait_recv()
            at = slice(cells + side * wide, cells + (side + 1) * wide)
            cotm[at, :] = cot_recv[side].astype(F32) * mask[at, :]

    w_parts = math.gcd(tap_rows // 16, s_count)
    w_rows = tap_rows // w_parts
    w_mine = s % w_parts
    w_group = s - w_mine

    def wz_copy(which, k):
        at = pl.ds(w_mine * w_rows, w_rows)
        slot = n - k - 1
        return pltpu.make_async_remote_copy(
            src_ref=wv.at[which, (z + k) % n, at, :], dst_ref=wf.at[which, slot, at, :],
            send_sem=wz_ssem.at[which, slot], recv_sem=wz_rsem.at[which, slot],
            device_id=((z + k) % n, s), device_id_type=MESH)

    def wp_copy(which, slot, k, whose):
        at = pl.ds(whose * w_rows, w_rows)
        return pltpu.make_async_remote_copy(
            src_ref=wf.at[which, slot, at, :], dst_ref=wf.at[which, slot, at, :],
            send_sem=wp_ssem.at[which, slot, k], recv_sem=wp_rsem.at[which, slot, whose],
            device_id=(z, w_group + (w_mine + k) % w_parts), device_id_type=MESH)

    def weights_over_z(which):
        for copy in w_copies[which * n:(which + 1) * n]:
            copy.wait()

        @pl.loop(1, n)
        def _(k):
            wz_copy(which, k).start()

    def slot_of(block):
        return (block - z + n - 1) % n

    def weights_round(which):
        @pl.loop(1, n)
        def _(distance):
            for sign in (1, -1):
                block = z - distance * sign

                @pl.when((block >= 0) & (block < n))
                def _():
                    slot = slot_of(block)
                    wz_copy(which, n - 1 - slot).wait_recv()

                    @pl.loop(1, w_parts)
                    def _(k):
                        wp_copy(which, slot, k, w_mine).start()

    def weights_arrived(which, slot):
        @pl.loop(1, w_parts)
        def _(k):
            wp_copy(which, slot, k, (w_mine + k) % w_parts).wait_recv()

    def row_copy(slot, side):
        return pltpu.make_async_remote_copy(
            src_ref=row_send.at[slot, side], dst_ref=row_recv.at[slot, 1 - side],
            send_sem=row_ssem.at[slot, side], recv_sem=row_rsem.at[slot, 1 - side],
            device_id=(z, before if side == 0 else after), device_id_type=MESH)

    def send_rows(slot, ref):
        for side, start in ((0, 0), (1, cells - wide)):
            row_send[slot, side] = ref[start:start + wide, :]
            row_copy(slot, side).start()

    def take_rows(slot, ref):
        for side in range(2):
            row_copy(slot, 1 - side).wait_recv()
            ref[cells + side * wide:cells + (side + 1) * wide, :] = row_recv[slot, side]

    def st_copy(slot, k, whose):
        return pltpu.make_async_remote_copy(
            src_ref=st_send.at[slot], dst_ref=st_recv.at[slot, whose],
            send_sem=st_ssem.at[slot, k], recv_sem=st_rsem.at[slot, whose],
            device_id=(z, (s + k) % s_count), device_id_type=MESH)

    def send_stats(slot, values):
        for i, v in enumerate(values):
            st_send[slot, i:i + 1, :] = v
        for k in range(1, s_count):
            st_copy(slot, k, s).start()
        st_recv[slot, s] = st_send[slot]

    def take_stats(slot):
        for k in range(1, s_count):
            st_copy(slot, k, (s + k) % s_count).wait_recv()

    strip = 8
    column = lax.broadcasted_iota(jnp.int32, (strip * wide, ch), 0) % wide

    def shift(target, first, count):
        size = count * wide
        where = column[:size]
        here = pad[pl.ds(8 + first * wide, size), :]
        left = jnp.where(where == 0, 0.0, pad[pl.ds(7 + first * wide, size), :])
        right = jnp.where(where == wide - 1, 0.0, pad[pl.ds(9 + first * wide, size), :])
        for b, v in enumerate((left, here, right)):
            target[pl.ds(first, count), :, b * ch:(b + 1) * ch] = v.astype(BF16).reshape(count, wide, ch)

    edge = 2 * wide
    ag_rows = ((0, edge + packed), (edge + packed, packed))
    band_rows = rows // HALVES

    def unpack_half(ph, block, q, target):
        if q == 0:
            pad[8:8 + wide, :] = hold[ph, block, 0:wide, :].astype(F32)
            pad[8 + wide + cells:8 + 2 * wide + cells, :] = hold[ph, block, wide:edge, :].astype(F32)
            shift(target, 0, 1)
            shift(target, rows + 1, 1)
        for j in range(2):
            start = edge + q * packed + j * (packed - unpack.shape[3])
            at = 8 + wide + q * band + j * (band // 2)
            pad[at:at + band // 2, :] = dot(unpack[q, j], hold[ph, block, start:start + unpack.shape[3], :])

        for i in range(band_rows // strip):
            shift(target, 1 + q * band_rows + i * strip, strip)

    def add_conv(q, field, taps, turned_taps=None):
        first, last = (0, band_rows - 1) if q == 0 else (band_rows - 1, rows)
        count = last - first
        size = (count + 2) * wide
        lhs = jnp.concatenate([
            field[first + i:last + 2 + i, :, :].reshape(size, 3 * ch) for i in range(2)], axis=1)
        if turned_taps is None:
            none = jnp.zeros((3 * ch, ch), BF16)
            rhs = jnp.concatenate([
                jnp.concatenate([taps(0), taps(2)], axis=1), jnp.concatenate([taps(1), none], axis=1)], axis=0)
            value = dot(lhs, rhs)
        else:
            def row_taps(a):
                return [turned_taps(3 * (2 - a) + 2 - b) for b in range(3)]
            none = jnp.zeros((ch, 3 * ch), BF16)
            rhs = jnp.concatenate([
                jnp.concatenate(row_taps(0) + row_taps(1), axis=1), jnp.concatenate(row_taps(2) + [none], axis=1)], axis=0)
            value = lax.dot_general(lhs, rhs, (((1,), (1,)), ((), ())), preferred_element_type=F32)
        at = pl.ds(first * wide, count * wide)
        acc[at, :] = acc[at, :] + value[0:count * wide, 0:ch] + value[2 * wide:size, ch:2 * ch]

    def ag_copy(ph, block, q, sign):
        at = pl.ds(*ag_rows[q])
        return pltpu.make_async_remote_copy(
            src_ref=hold.at[ph, block, at, :], dst_ref=hold.at[ph, block, at, :],
            send_sem=ag_ssem.at[ph, (1 - sign) // 2, block, q], recv_sem=ag_rsem.at[ph, block, q],
            device_id=(z + sign, s), device_id_type=MESH)

    def pack_field(ph, source, fill=None, first=None):
        if fill is not None:
            fill(cells, edge, 0)
        hold[ph, z, 0:edge, :] = source[cells:cells + edge, :].astype(BF16)
        for q in range(HALVES):
            if first is not None:
                first(q)
            if fill is not None:
                chunked(fill, 0, q * band, band)
            hold[ph, z, edge + q * packed:edge + (q + 1) * packed, :] = dot(
                pack[q], source[q * band:(q + 1) * band, :].astype(BF16)).astype(BF16)
            for sign in (1, -1):
                @pl.when((z + sign >= 0) & (z + sign < n))
                def _():
                    ag_copy(ph, z, q, sign).start()

    def inside(slice_at):
        return (slice_at >= 0) & (slice_at < n)

    def take_and_pass(ph, k, q, sign, passes=True, takes=True):
        block = z - k * sign

        @pl.when((k > 0) & inside(block))
        def _():
            if passes and takes:
                ag_copy(ph, block, q, sign).wait_recv()

            @pl.when(inside(z + sign))
            def _():
                if passes:
                    if not takes:
                        ag_copy(ph, block, q, sign).wait_recv()
                    ag_copy(ph, block, q, sign).start()

            if not passes:
                @pl.when(jnp.logical_not(inside(z + sign)))
                def _():
                    ag_copy(ph, block, q, sign).wait_recv()

    near = jnp.where(z < n - n // 2, 1, 0)

    def consume_way(k, q, way, consume):
        block = z - k * (1 - 2 * way)

        @pl.when((k >= 0) & (k < n) & inside(block) & ((k > 0) | (way == near)))
        def _():
            consume(k, block, q)

    def take_both(ph, k, q, **how):
        @pl.loop(0, 2)
        def _(i):
            way = (near + i) % 2
            take_and_pass(ph, k, q, 1 - 2 * way, **how)

    def gather(ph, consume, each):
        @pl.loop(0, n)
        def _(k):
            for q in range(HALVES):
                take_both(ph, k, q)
                if q:
                    consume_way(k, q - 1, 1 - near, consume)
                else:
                    consume_way(k - 1, HALVES - 1, 1 - near, consume)
                consume_way(k, q, near, consume)
            each(k)

    def gather_passing_first(ph, consume, each):
        @pl.loop(0, n)
        def _(k):
            @pl.when(k == 1)
            def _():
                @pl.loop(1, n)
                def _(ahead):
                    for q in range(HALVES):
                        take_both(ph, ahead, q, takes=False)
            for q in range(HALVES):
                take_both(ph, k, q, passes=False)

                @pl.loop(0, 2)
                def _(i):
                    consume_way(k, q, (near + i) % 2, consume)
            each(k)

    last_pass = jnp.maximum(jnp.where(z < n - 1, z, 0), jnp.where(z > 0, n - 1 - z, 0))

    def forward(ph, field):
        def consume(k, block, q):
            into = taken.at[block]
            unpack_half(ph, block, q, into)

            @pl.when(k == 0)
            def _():
                add_conv(q, into, lambda a: wv[ph, z, 3 * a * ch:3 * (a + 1) * ch, :])

            @pl.when(k > 0)
            def _():
                slot = slot_of(block)
                if q == 0:
                    weights_arrived(ph, slot)
                add_conv(q, into, lambda a: wf[ph, slot, 3 * a * ch:3 * (a + 1) * ch, :])

        def each(k):
            if ph == 0:
                @pl.when(k == 0)
                def _():
                    weights_round(0)

                @pl.when(k == 1)
                def _():
                    weights_over_z(1)
        (gather if ph else gather_passing_first)(ph, consume, each)

    def turn_field(ph, field):
        main = [field[start:start + ch, :].T for start in range(0, cells, ch)]
        ends = field[cells:cells + edge, :]
        if edge < ch:
            ends = jnp.concatenate([ends, jnp.zeros((ch - edge, ch), F32)], axis=0)
        ends = ends.T
        for i, here in enumerate(main):
            left = jnp.concatenate(
                [ends[:, 0:wide] if i == 0 else main[i - 1][:, ch - wide:], here[:, 0:ch - wide]], axis=1)
            right = jnp.concatenate(
                [here[:, wide:], main[i + 1][:, 0:wide] if i + 1 < len(main) else ends[:, wide:edge]], axis=1)
            for a, v in enumerate((left, here, right)):
                x_t[ph, a * ch:(a + 1) * ch, i * ch:(i + 1) * ch] = v.astype(BF16)

    half_rows = tap_rows // 2
    owners = math.gcd(half_rows // 16, chips)
    piece = half_rows // owners

    def c_copy(ph, j):
        return pltpu.make_async_remote_copy(
            src_ref=psend.at[ph, j], dst_ref=crecv.at[ph, j],
            send_sem=c_ssem.at[ph, j], recv_sem=c_rsem.at[ph, j],
            device_id=(z, chip * 2 + 1 - core), device_id_type=MESH)

    def q_copy(ph, j, e, whose, owner):
        return pltpu.make_async_remote_copy(
            src_ref=hsend.at[ph, j, owner], dst_ref=qrecv.at[ph, j, whose],
            send_sem=q_ssem.at[ph, j, e], recv_sem=q_rsem.at[ph, j, whose],
            device_id=(z, ((chip + e) % chips) * 2 + core), device_id_type=MESH)

    def f_copy(ph, j, e, owner):
        return pltpu.make_async_remote_copy(
            src_ref=wout.at[ph, j, core, owner], dst_ref=wout.at[ph, j, core, owner],
            send_sem=f_ssem.at[ph, j, e], recv_sem=f_rsem.at[ph, j, owner],
            device_id=(z, ((chip + e) % chips) * 2 + core), device_id_type=MESH)

    def h_copy(ph, j, whose):
        return pltpu.make_async_remote_copy(
            src_ref=wout.at[ph, j, whose], dst_ref=wout.at[ph, j, whose],
            send_sem=h_ssem.at[ph, j], recv_sem=h_rsem.at[ph, j],
            device_id=(z, chip * 2 + 1 - core), device_id_type=MESH)

    def o_copy(ph, j):
        target = (out_wg1, out_wg2)[ph]
        if aligned:
            target = target.at[:, :, :, pl.ds(pl.multiple_of(j * ch, ch), ch)]
        else:
            target = target.at[j]
        return pltpu.make_async_copy(wout.at[ph, j], target, o_sem.at[ph, j])

    def sum_cores(ph, j):
        for o in range(owners):
            psend[ph, j, o] = part[ph, j, 1 - core, o].astype(BF16)
        c_copy(ph, j).start()

    def sum_chips(ph, j):
        c_copy(ph, j).wait_recv()
        for o in range(owners):
            v = part[ph, j, core, o] + crecv[ph, j, o].astype(F32)
            part[ph, j, core, o] = v
            hsend[ph, j, o] = v.astype(BF16)

        @pl.loop(1, chips)
        def _(e):
            peer = (chip + e) % chips

            @pl.when(peer < owners)
            def _():
                q_copy(ph, j, e, chip, peer).start()

    def spread_chips(ph, j):
        @pl.when(chip < owners)
        def _():
            @pl.loop(1, chips)
            def _(e):
                q_copy(ph, j, e, (chip + e) % chips, chip).wait_recv()
            v = part[ph, j, core, chip]
            for e in range(1, chips):
                v = v + qrecv[ph, j, (chip + e) % chips].astype(F32)
            wout[ph, j, core, chip] = v.astype(BF16)

            @pl.loop(1, chips)
            def _(e):
                f_copy(ph, j, e, chip).start()

    def spread_cores(ph, j):
        @pl.loop(1, chips)
        def _(e):
            peer = (chip + e) % chips

            @pl.when(peer < owners)
            def _():
                f_copy(ph, j, e, peer).wait_recv()
        h_copy(ph, j, core).start()

    def finish(ph, j):
        h_copy(ph, j, 1 - core).wait_recv()
        o_copy(ph, j).start()

    def put_part(ph, j, tap, value):
        start = tap * ch
        done = 0
        while done < ch:
            row = start + done
            side, o, at = row // half_rows, row % half_rows // piece, row % piece
            size = min(ch - done, piece - at)
            part[ph, j, side, o, at:at + size, :] = value[done:done + size, :]
            done += size

    stages = (sum_cores, sum_chips, spread_chips, spread_cores, finish)

    def of_step(k, fn):
        @pl.loop(0, 2)
        def _(way):
            block = z - k * (1 - 2 * way)

            @pl.when((k >= 0) & (k < n) & inside(block) & ((k > 0) | (way == 0)))
            def _():
                fn(block)

    passing = last_pass > 0

    def made_at(step):
        first = jnp.where(passing & (step > 0), jnp.where(step == last_pass, 1, step + 1), step)
        return first, step + 1

    def advance(ph, k):
        for age in range(1, len(stages)):
            step = k - age

            @pl.when((step >= 0) & (step < n))
            def _():
                @pl.loop(*made_at(step))
                def _(made):
                    of_step(made, functools.partial(stages[age], ph))

    def advance_all(ph, age):
        @pl.loop(0, n)
        def _(j):
            stages[age](ph, j)

    def field_grad(ph, block):
        grad = taken[block, 1:rows + 1, :, :].reshape(cells, 3 * ch)
        value = dot(x_t[ph], grad)
        for a in range(3):
            for b in range(3):
                put_part(ph, block, 3 * a + b, value[a * ch:(a + 1) * ch, (2 - b) * ch:(3 - b) * ch])

    def make_grad(ph, block):
        field_grad(ph, block)
        sum_cores(ph, block)

    def backward(ph):
        last = ph == 0

        def consume(k, block, q):
            into = taken.at[block]
            unpack_half(2 + ph, block, q, into)
            if last and q == HALVES - 1:
                @pl.when((k == 0) | (k >= last_pass))
                def _():
                    make_grad(ph, block)
            add_conv(q, into, None, lambda t: wv[ph, block, t * ch:(t + 1) * ch, :])

        def each(k):
            first, end = made_at(k)
            if last:
                @pl.loop(first, end - 1)
                def _(step):
                    of_step(step, functools.partial(make_grad, ph))
                advance(ph, k)
                for age in range(2, len(stages)):
                    @pl.when(k == age - 2)
                    def _():
                        advance_all(1, age)
            else:
                @pl.loop(first, jnp.where(passing | (k < n - 2), end, first))
                def _(step):
                    of_step(step, functools.partial(make_grad, ph))
        gather(2 + ph, consume, each)

    def fold(v):
        return jnp.sum(v.reshape(v.shape[0] // 8, 8, ch), axis=0)

    def flatten(v):
        return jnp.sum(v, axis=0, keepdims=True)

    zero = jnp.zeros((8, ch), F32)

    def local_moments(ref):
        def sums(start, size, carry):
            at = pl.ds(start, size)
            m = mask[at, :]
            return carry[0] + fold(ref[at, :] * m), carry[1] + fold(m)
        added, number = (flatten(v) for v in chunked(sums, (zero, zero)))
        middle = added / jnp.maximum(number, 1.0)

        def spread(start, size, carry):
            at = pl.ds(start, size)
            c = (ref[at, :] - middle) * mask[at, :]
            return carry + fold(c * c)
        return added, number, flatten(chunked(spread, zero))

    def moments(slot):
        take_stats(slot)
        got = [st_recv[slot, k] for k in range(s_count)]
        added = sum(g[0:1] for g in got)
        number = sum(g[1:2] for g in got)
        mean = added / number
        spread = 0.0
        for g in got:
            off = g[0:1] / jnp.maximum(g[1:2], 1.0) - mean
            spread = spread + (g[2:3] + g[1:2] * off * off)
        return mean, lax.rsqrt(spread / number + EPSILON), number

    def everywhere(fn):
        chunked(fn, 0)
        fn(cells, 2 * wide, 0)

    gain1, shift1, gain2, shift2 = (r[...] for r in (gain1_in, shift1_in, gain2_in, shift2_in))

    weights_over_z(0)

    quarter = band // 2
    kept = packed // 2
    window = unpack.shape[3]
    below = lax.broadcasted_iota(jnp.int32, (quarter, quarter), 1) < lax.broadcasted_iota(jnp.int32, (quarter, quarter), 0)
    below = below.astype(F32).astype(BF16)

    def make_pack(h):
        for j in range(2):
            lv = mask[h * band + j * quarter:h * band + (j + 1) * quarter, :]
            place = jnp.where(lv > 0.0, dot(below, lv.astype(BF16)) + j * kept, -1.0)
            places[h, j] = place
            across = place.T[0:1, :]
            spot = lax.broadcasted_iota(jnp.int32, (packed, quarter), 0).astype(F32)
            pack[h, :, j * quarter:(j + 1) * quarter] = jnp.where(spot == across, 1.0, 0.0).astype(BF16)

    def make_unpack(h):
        for j in range(2):
            for start in range(0, window, ch):
                size = min(ch, window - start)
                spot = start + j * (packed - window) + lax.broadcasted_iota(jnp.int32, (quarter, size), 1)
                unpack[h, j, :, start:start + size] = jnp.where(
                    places[h, j, :, :size] == spot.astype(F32), 1.0, 0.0).astype(BF16)

    for side in range(2):
        edge_copy(1 - side).wait_recv()
        there = jnp.where(s > 0, 1.0, 0.0) if side == 0 else jnp.where(s < s_count - 1, 1.0, 0.0)
        at = slice(cells + side * wide, cells + (side + 1) * wide)
        masked[at, :] = edge_recv[side, 0].astype(F32) * there
        mask[at, :] = edge_recv[side, 1].astype(F32) * there

    pack_field(0, masked, first=make_pack)
    for h in range(HALVES):
        make_unpack(h)
    forward(0, masked)
    send_rows(0, acc)
    send_stats(0, local_moments(acc))
    weights_round(1)
    load_cotangent()
    mean1, scale1, count = moments(0)

    def activate_one(start, size, carry):
        at = pl.ds(start, size)
        main = start is not cells
        nv = ((acc if main else normed1)[at, :] - mean1) * scale1
        normed1[at, :] = nv
        hid[at, :] = gelu_parts(nv * gain1 + shift1)[0] * mask[at, :]
        if main:
            acc[at, :] = jnp.zeros((size, ch), F32)
        return carry

    def slope_one(start, size, carry):
        at = pl.ds(start, size)
        slope1[at, :] = gelu_parts(normed1[at, :] * gain1 + shift1)[1] * mask[at, :]
        return carry

    take_rows(0, normed1)
    pack_field(1, hid, activate_one)
    everywhere(slope_one)
    forward(1, hid)
    send_rows(1, acc)
    send_stats(1, local_moments(acc))
    turn_field(0, masked)
    turn_field(1, hid)
    mean2, scale2, _ = moments(1)

    def activate_two(source, start, size):
        at = pl.ds(start, size)
        nv = (source[at, :] - mean2) * scale2
        normed2[at, :] = nv
        value, slope = gelu_parts(nv * gain2 + shift2 + masked[at, :])
        t = cotm[at, :] * slope
        through[at, :] = t
        return value, nv, t

    def activate_main(start, size, carry):
        value, nv, t = activate_two(acc, start, size)
        at = pl.ds(start, size)
        hid2[at, :] = value * mask[at, :]
        acc[at, :] = jnp.zeros((size, ch), F32)
        return carry[0] + fold(t * nv), carry[1] + fold(t)

    send_stats(2, [flatten(v) for v in chunked(activate_main, (zero, zero))])
    take_rows(1, normed2)
    take_cotangent()
    activate_two(normed2, cells, edge)
    to_flat(hid2, out_block)

    def gradient_sums(slot):
        take_stats(slot)
        got = [st_recv[slot, k] for k in range(s_count)]
        return sum(g[0:1] for g in got), sum(g[1:2] for g in got)

    def norm_back(upstream, normed, gain, scale, sums):
        gain_grad, shift_grad = sums
        factor = gain * scale
        level, tilt = shift_grad / count, gain_grad / count

        def fill(start, size, carry):
            at = pl.ds(start, size)
            v = upstream[at, :] - mask[at, :] * (level + normed[at, :] * tilt)
            hid[at, :] = factor * v
            return carry
        return fill

    sums2 = gradient_sums(2)
    pack_field(3, hid, norm_back(through, normed2, gain2, scale2, sums2))
    backward(1)

    send_rows(2, acc)

    def inner_main(start, size, carry):
        at = pl.ds(start, size)
        v = acc[at, :] * slope1[at, :]
        slope1[at, :] = v
        acc[at, :] = jnp.zeros((size, ch), F32)
        return carry[0] + fold(v * normed1[at, :]), carry[1] + fold(v)

    send_stats(3, [flatten(v) for v in chunked(inner_main, (zero, zero))])

    @pl.when(jnp.logical_not(passing))
    def _():
        for step in range(n - 2, n):
            of_step(step, functools.partial(make_grad, 1))
    for side in range(2):
        row_copy(2, 1 - side).wait_recv()
        at = slice(cells + side * wide, cells + (side + 1) * wide)
        slope1[at, :] = row_recv[2, side] * slope1[at, :]
    sums1 = gradient_sums(3)
    pack_field(2, hid, norm_back(slope1, normed1, gain1, scale1, sums1))
    advance_all(1, 1)
    backward(0)
    advance(0, n)

    def finish_input(start, size, carry):
        at = pl.ds(start, size)
        acc[at, :] = (acc[at, :] + through[at, :]) * mask[at, :]
        return carry

    chunked(finish_input, 0)
    to_flat(acc, out_input)
    out_gain1[...], out_shift1[...] = sums1
    out_gain2[...], out_shift2[...] = sums2
    for extra in range(1, len(stages) - 1):
        advance(0, n + extra)

    for side in range(2):
        edge_copy(side).wait_send()
        cot_copy(side).wait_send()
        for slot in range(3):
            row_copy(slot, side).wait_send()

    @pl.loop(1, s_count)
    def _(k):
        for slot in range(4):
            st_copy(slot, k, s).wait_send()

    @pl.loop(1, n)
    def _(k):
        for which in range(2):
            wz_copy(which, k).wait_send()

    @pl.loop(1, w_parts)
    def _(k):
        for which in range(2):
            for slot in range(n - 1):
                wp_copy(which, slot, k, w_mine).wait_send()

    @pl.loop(0, n)
    def _(k):
        for sign in (1, -1):
            block = z - k * sign

            @pl.when((block >= 0) & (block < n) & (z + sign >= 0) & (z + sign < n))
            def _():
                for ph in range(4):
                    for q in range(HALVES):
                        ag_copy(ph, block, q, sign).wait_send()

    @pl.loop(0, n)
    def _(j):
        for ph in range(2):
            c_copy(ph, j).wait_send()
            h_copy(ph, j, core).wait_send()
            o_copy(ph, j).wait()

            @pl.loop(1, chips)
            def _(e):
                peer = (chip + e) % chips

                @pl.when(peer < owners)
                def _():
                    q_copy(ph, j, e, chip, peer).wait_send()

                @pl.when(chip < owners)
                def _():
                    f_copy(ph, j, e, chip).wait_send()


def finish_kernel(count, *refs):
    ins, outs = refs[:count], refs[count:2 * count]
    narrow, wide, in_sem, out_sem, take_sem, give_sem = refs[2 * count:2 * count + 6]
    held = refs[2 * count + 6:]
    rows = narrow.shape[1] // FINISH_PARTS
    parts = [(w, i, pl.ds(i * rows, rows)) for i in range(FINISH_PARTS) for w in range(2)]
    loads = [pltpu.make_async_copy(ins[w].at[at, :], narrow.at[w, at, :], in_sem.at[w, i]) for w, i, at in parts]
    stores = [pltpu.make_async_copy(wide.at[w, at, :], outs[w].at[at, :], out_sem.at[w, i]) for w, i, at in parts]
    takes = [pltpu.make_async_copy(ins[2 + k], v, take_sem.at[k]) for k, v in enumerate(held)]
    gives = [pltpu.make_async_copy(v, outs[2 + k], give_sem.at[k]) for k, v in enumerate(held)]
    for copy in loads + takes:
        copy.start()
    for load, store, (w, i, at) in zip(loads, stores, parts):
        load.wait()
        wide[w, at, :] = narrow[w, at, :].astype(F32)
        store.start()
    for take, give in zip(takes, gives):
        take.wait()
        give.start()
    for copy in stores + gives:
        copy.wait()


def per_device(n, s_count, blocks, weight_one, weight_two, gain_one, shift_one, gain_two, shift_two, cell_live, cotangent):
    rows, wide = cell_live.shape
    ch = blocks.shape[1] // wide
    cells = rows * wide
    total = cells + 2 * wide
    packed = 2 * -(-most_live(rows // HALVES // 2, wide) // 8) * 8
    aligned = ch % 128 == 0
    chips = s_count // 2
    tap_rows = 9 * ch
    half_rows = tap_rows // 2
    owners = math.gcd(half_rows // 16, chips)
    piece = half_rows // owners

    if aligned:
        weight_one, weight_two = (w.reshape(tap_rows, n * ch) for w in (weight_one, weight_two))
    else:
        weight_one, weight_two = (
            w.reshape(tap_rows, n, ch).transpose(1, 0, 2) for w in (weight_one, weight_two))
    grad_shape = (2, owners, piece, n * ch) if aligned else (n, 2, owners, piece, ch)
    vmem = pl.BlockSpec(memory_space=pltpu.VMEM)
    hbm = pl.BlockSpec(memory_space=pl.ANY)
    sem = pltpu.SemaphoreType.DMA
    field = pltpu.VMEM((total, ch), F32)
    scratch = [
        pltpu.VMEM((ch * wide, 128), F32),
        pltpu.VMEM((2, n, tap_rows, ch), BF16),
        pltpu.VMEM((2, n - 1, tap_rows, ch), BF16),
        pltpu.VMEM((2, 3 * ch, cells), BF16),
        pltpu.VMEM((HALVES, packed, cells // HALVES), BF16),
        pltpu.VMEM((HALVES, 2, cells // HALVES // 2, -(-packed // 2 // 16) * 16), BF16),
        pltpu.VMEM((HALVES, 2, cells // HALVES // 2, ch), F32),
        pltpu.VMEM((2, 2, wide, ch), BF16),
        pltpu.VMEM((2, 2, wide, ch), BF16),
        pltpu.VMEM((2, wide, ch), BF16),
        pltpu.VMEM((2, wide, ch), BF16),
        field, field, field, field, field, field, field, field, field,
        pltpu.VMEM((total + 16, ch), F32),
        pltpu.VMEM((cells, ch), F32),
        pltpu.VMEM((4, n, 2 * wide + HALVES * packed, ch), BF16),
        pltpu.VMEM((n, rows + 3, wide, 3 * ch), BF16),
        pltpu.VMEM((2, n, 2, owners, piece, ch), F32),
        pltpu.VMEM((2, n, owners, piece, ch), BF16),
        pltpu.VMEM((2, n, owners, piece, ch), BF16),
        pltpu.VMEM((2, n, owners, piece, ch), BF16),
        pltpu.VMEM((2, n, chips, piece, ch), BF16),
        pltpu.VMEM((2, n, 2, owners, piece, ch), BF16),
        pltpu.VMEM((4, 8, ch), F32),
        pltpu.VMEM((4, s_count, 8, ch), F32),
        pltpu.VMEM((3, 2, wide, ch), F32),
        pltpu.VMEM((3, 2, wide, ch), F32),
        sem((2, n)),
        sem((2, n)), sem((2, n)),
        sem((2, n - 1, s_count)), sem((2, n - 1, s_count)),
        sem((2,)), sem((2,)),
        sem((2,)), sem((2,)),
        sem((4, 2, n, HALVES)), sem((4, n, HALVES)),
        sem((4, s_count)), sem((4, s_count)),
        sem((3, 2)), sem((3, 2)),
        sem((2, n)), sem((2, n)),
        sem((2, n, chips)), sem((2, n, chips)),
        sem((2, n, chips)), sem((2, n, chips)),
        sem((2, n)), sem((2, n)),
        sem((2, n)),
    ]
    block_out, input_grad, wg1, wg2, *sums = pl.pallas_call(
        functools.partial(block_kernel, n, s_count, rows, wide, ch, aligned, packed),
        out_shape=(
            jax.ShapeDtypeStruct((rows, ch * wide), BF16),
            jax.ShapeDtypeStruct((rows, ch * wide), F32),
            jax.ShapeDtypeStruct(grad_shape, BF16),
            jax.ShapeDtypeStruct(grad_shape, BF16),
            *[jax.ShapeDtypeStruct((1, ch), F32)] * 4,
        ),
        in_specs=[vmem] * 7 + [hbm] * 2,
        out_specs=(vmem, vmem, hbm, hbm, vmem, vmem, vmem, vmem),
        scratch_shapes=scratch,
        compiler_params=pltpu.CompilerParams(
            collective_id=0, has_side_effects=True, vmem_limit_bytes=60 * 1024 * 1024),
    )(blocks, cotangent, cell_live.T,
      *(v.reshape(1, ch) for v in (gain_one, shift_one, gain_two, shift_two)), weight_one, weight_two)

    if not aligned:
        def whole(grad):
            grad = grad.reshape(n, tap_rows, ch).transpose(1, 0, 2)
            return grad.astype(F32).reshape(9, ch, n * ch)
        return (block_out, input_grad, whole(wg1), whole(wg2), *(v.reshape(ch) for v in sums))

    wg1, wg2 = (w.reshape(tap_rows, n * ch) for w in (wg1, wg2))
    wide_grad = jax.ShapeDtypeStruct((tap_rows, n * ch), F32)
    moved = (block_out, input_grad, *sums)
    grad1, grad2, *moved = pl.pallas_call(
        functools.partial(finish_kernel, 2 + len(moved)),
        out_shape=(wide_grad, wide_grad, *(jax.ShapeDtypeStruct(v.shape, v.dtype) for v in moved)),
        in_specs=[pl.BlockSpec(memory_space=pl.ANY)] * (2 + len(moved)),
        out_specs=[pl.BlockSpec(memory_space=pl.ANY)] * (2 + len(moved)),
        scratch_shapes=[
            pltpu.VMEM((2, tap_rows, n * ch), BF16), pltpu.VMEM((2, tap_rows, n * ch), F32),
            sem((2, FINISH_PARTS)), sem((2, FINISH_PARTS)), sem((len(moved),)), sem((len(moved),)),
            *(pltpu.VMEM(v.shape, v.dtype) for v in moved),
        ],
        compiler_params=pltpu.CompilerParams(vmem_limit_bytes=64 * 1024 * 1024),
    )(wg1, wg2, *moved)
    block_out, input_grad, *sums = moved
    grads = (g.reshape(9, ch, n * ch) for g in (grad1, grad2))
    return (block_out, input_grad, *grads, *(v.reshape(ch) for v in sums))


def solution(mesh):
    return jax.shard_map(
        functools.partial(per_device, mesh.shape["chan"], mesh.shape["space"]),
        mesh=mesh,
        in_specs=(
            P("space", "chan"),
            P(None, "chan", None),
            P(None, "chan", None),
            P("chan"),
            P("chan"),
            P("chan"),
            P("chan"),
            P("space", None),
            P("space", "chan"),
        ),
        out_specs=(
            P("space", "chan"),
            P("space", "chan"),
            P(None, "chan", None),
            P(None, "chan", None),
            P("chan"),
            P("chan"),
            P("chan"),
            P("chan"),
        ),
        check_vma=False,
    )
```

profile of v0, /device:TPU:1, one launch (start us, length us, event | category | flops | bytes accessed | tf_op | source)
XLA Modules:
  0.0 117.2 jit_solution(6798580079231414180)
XLA Ops:
  0.6 112.7 %shard_map.152 = (bf16[64,2048]{1,0:T(8,128)(2,1)}, f32[64,2048]{1,0:T(8,128)}, bf16[2,4,144,512]{3,2,1,0:T(8,128)(2,1)}, bf16[2,4,144,512]{3,2,1,0:T(8,128)(2,1...) custom-call(bf16[64,2048]{1,0:T(8,128)(2,1)} %refs_0_.1, ...), custom_call_target="tpu_custom_call" | custom-call | tf_op jit(solution)/shard_map/pallas_call | solution.py:925
  113.3 3.7 %shard_map.153 = (f32[1152,512]{1,0:T(8,128)}, f32[1152,512]{1,0:T(8,128)}, bf16[64,2048]{1,0:T(8,128)(2,1)}, f32[64,2048]{1,0:T(8,128)}, f32[1,128]{1,0:T(1,128...) custom-call(bf16[1152,512]{1,0:T(8,128)(2,1)} %bitcast.17, bf16[1152,512]{1,0:T(8,128)(2,1)} %bitcast.18, ...), custom_call_target="tpu_custom_call" | custom-call | tf_op jit(solution)/shard_map/pallas_call | solution.py:951
where the time goes:
time: 117 us
  Pallas kernels  116 us (99%)
    pallas_call x1, Pallas kernels, per_device(): pl.pallas_call(functools.partial(block_kernel, n, s_count, rows, wide, ch...  113 us
    pallas_call x1, Pallas kernels, per_device(): pl.pallas_call(functools.partial(finish_kernel, 2 + len(moved)), out_shap...  3.68 us

commit v1 on v0

--- a/solution.py
+++ b/solution.py
@@ -15,7 +15,7 @@
 ROOT_HALF = 0.7071067811865476
 ROOT_TWO_PI = 0.3989422804014327
 CHUNK = 64
-FINISH_PARTS = 4
+FINISH_PARTS = 8
 UNROLL = 2
 HALVES = 2
 LARGE, SMALL = 7, 3
@@ -42,10 +42,10 @@
     (out_block, out_input, out_wg1, out_wg2, out_gain1, out_shift1, out_gain2, out_shift2) = refs[9:17]
     (turned, wv, wf, x_t, pack, unpack, places, edge_send, edge_recv, cot_send, cot_recv, cotm, mask, masked,
      normed1, normed2, through, slope1, hid, hid2, pad, acc, hold, taken,
-     part, psend, crecv, hsend, qrecv, wout, st_send, st_recv, row_send, row_recv,
+     part, psend, crecv, hsend, qrecv, wout, st_send, st_recv, row_send, row_recv, flat_block, flat_input,
      w_sem, wz_ssem, wz_rsem, wp_ssem, wp_rsem, e_ssem, e_rsem, ce_ssem, ce_rsem, ag_ssem, ag_rsem,
      st_ssem, st_rsem, row_ssem, row_rsem, c_ssem, c_rsem, q_ssem, q_rsem,
-     f_ssem, f_rsem, h_ssem, h_rsem, o_sem) = refs[17:]
+     f_ssem, f_rsem, h_ssem, h_rsem, o_sem, r_sem) = refs[17:]
 
     z = lax.axis_index("chan")
     s = lax.axis_index("space")
@@ -412,6 +412,10 @@
                 @pl.when(k == 1)
                 def _():
                     weights_over_z(1)
+
+                @pl.when(k == last_pass)
+                def _():
+                    load_cotangent()
         (gather if ph else gather_passing_first)(ph, consume, each)
 
     def turn_field(ph, field):
@@ -590,7 +594,7 @@
                     def _():
                         advance_all(1, age)
             else:
-                @pl.loop(first, jnp.where(passing | (k < n - 2), end, first))
+                @pl.loop(first, jnp.where(passing | (k < n - 1), end, first))
                 def _(step):
                     of_step(step, functools.partial(make_grad, ph))
         gather(2 + ph, consume, each)
@@ -667,6 +671,53 @@
         masked[at, :] = edge_recv[side, 0].astype(F32) * there
         mask[at, :] = edge_recv[side, 1].astype(F32) * there
 
+    def stats_sent(slot):
+        for k in range(1, s_count):
+            st_copy(slot, k, s).wait_send()
+
+    def row_sent(slot):
+        for side in range(2):
+            row_copy(slot, side).wait_send()
+
+    def gathered_sent(ph):
+        @pl.loop(0, n)
+        def _(k):
+            for sign in (1, -1):
+                block = z - k * sign
+
+                @pl.when(inside(block) & inside(z + sign))
+                def _():
+                    for q in range(HALVES):
+                        ag_copy(ph, block, q, sign).wait_send()
+
+    def weights_sent(which):
+        for k in range(1, n):
+            wz_copy(which, k).wait_send()
+
+        @pl.loop(1, w_parts)
+        def _(k):
+            for slot in range(n - 1):
+                wp_copy(which, slot, k, w_mine).wait_send()
+
+    def grads_sent(ph):
+        @pl.loop(0, n)
+        def _(j):
+            c_copy(ph, j).wait_send()
+            h_copy(ph, j, core).wait_send()
+            o_copy(ph, j).wait()
+            for e in range(1, chips):
+                peer = (chip + e) % chips
+
+                @pl.when(peer < owners)
+                def _():
+                    q_copy(ph, j, e, chip, peer).wait_send()
+
+                @pl.when(chip < owners)
+                def _():
+                    f_copy(ph, j, e, chip).wait_send()
+
+    block_copy = pltpu.make_async_copy(flat_block, out_block, r_sem.at[0])
+
     pack_field(0, masked, first=make_pack)
     for h in range(HALVES):
         make_unpack(h)
@@ -674,7 +725,6 @@
     send_rows(0, acc)
     send_stats(0, local_moments(acc))
     weights_round(1)
-    load_cotangent()
     mean1, scale1, count = moments(0)
 
     def activate_one(start, size, carry):
@@ -700,6 +750,13 @@
     send_stats(1, local_moments(acc))
     turn_field(0, masked)
     turn_field(1, hid)
+    weights_sent(0)
+    gathered_sent(0)
+    stats_sent(0)
+    row_sent(0)
+    for side in range(2):
+        edge_copy(side).wait_send()
+        cot_copy(side).wait_send()
     mean2, scale2, _ = moments(1)
 
     def activate_two(source, start, size):
@@ -722,7 +779,10 @@
     take_rows(1, normed2)
     take_cotangent()
     activate_two(normed2, cells, edge)
-    to_flat(hid2, out_block)
+    to_flat(hid2, flat_block)
+    block_copy.start()
+    weights_sent(1)
+    gathered_sent(1)
 
     def gradient_sums(slot):
         take_stats(slot)
@@ -758,12 +818,15 @@
 
     @pl.when(jnp.logical_not(passing))
     def _():
-        for step in range(n - 2, n):
-            of_step(step, functools.partial(make_grad, 1))
+        of_step(n - 1, functools.partial(make_grad, 1))
     for side in range(2):
         row_copy(2, 1 - side).wait_recv()
         at = slice(cells + side * wide, cells + (side + 1) * wide)
         slope1[at, :] = row_recv[2, side] * slope1[at, :]
+    stats_sent(1)
+    row_sent(1)
+    stats_sent(2)
+    gathered_sent(3)
     sums1 = gradient_sums(3)
     pack_field(2, hid, norm_back(slope1, normed1, gain1, scale1, sums1))
     advance_all(1, 1)
@@ -776,63 +839,21 @@
         return carry
 
     chunked(finish_input, 0)
-    to_flat(acc, out_input)
+    to_flat(acc, flat_input)
+    input_copy = pltpu.make_async_copy(flat_input, out_input, r_sem.at[1])
+    input_copy.start()
     out_gain1[...], out_shift1[...] = sums1
     out_gain2[...], out_shift2[...] = sums2
     for extra in range(1, len(stages) - 1):
         advance(0, n + extra)
 
-    for side in range(2):
-        edge_copy(side).wait_send()
-        cot_copy(side).wait_send()
-        for slot in range(3):
-            row_copy(slot, side).wait_send()
-
-    @pl.loop(1, s_count)
-    def _(k):
-        for slot in range(4):
-            st_copy(slot, k, s).wait_send()
-
-    @pl.loop(1, n)
-    def _(k):
-        for which in range(2):
-            wz_copy(which, k).wait_send()
-
-    @pl.loop(1, w_parts)
-    def _(k):
-        for which in range(2):
-            for slot in range(n - 1):
-                wp_copy(which, slot, k, w_mine).wait_send()
-
-    @pl.loop(0, n)
-    def _(k):
-        for sign in (1, -1):
-            block = z - k * sign
-
-            @pl.when((block >= 0) & (block < n) & (z + sign >= 0) & (z + sign < n))
-            def _():
-                for ph in range(4):
-                    for q in range(HALVES):
-                        ag_copy(ph, block, q, sign).wait_send()
-
-    @pl.loop(0, n)
-    def _(j):
-        for ph in range(2):
-            c_copy(ph, j).wait_send()
-            h_copy(ph, j, core).wait_send()
-            o_copy(ph, j).wait()
-
-            @pl.loop(1, chips)
-            def _(e):
-                peer = (chip + e) % chips
-
-                @pl.when(peer < owners)
-                def _():
-                    q_copy(ph, j, e, chip, peer).wait_send()
-
-                @pl.when(chip < owners)
-                def _():
-                    f_copy(ph, j, e, chip).wait_send()
+    stats_sent(3)
+    row_sent(2)
+    gathered_sent(2)
+    grads_sent(1)
+    grads_sent(0)
+    block_copy.wait()
+    input_copy.wait()
 
 
 def finish_kernel(count, *refs):
@@ -908,6 +929,8 @@
         pltpu.VMEM((4, s_count, 8, ch), F32),
         pltpu.VMEM((3, 2, wide, ch), F32),
         pltpu.VMEM((3, 2, wide, ch), F32),
+        pltpu.VMEM((rows, ch * wide), BF16),
+        pltpu.VMEM((rows, ch * wide), F32),
         sem((2, n)),
         sem((2, n)), sem((2, n)),
         sem((2, n - 1, s_count)), sem((2, n - 1, s_count)),
@@ -921,6 +944,7 @@
         sem((2, n, chips)), sem((2, n, chips)),
         sem((2, n)), sem((2, n)),
         sem((2, n)),
+        sem((2,)),
     ]
     block_out, input_grad, wg1, wg2, *sums = pl.pallas_call(
         functools.partial(block_kernel, n, s_count, rows, wide, ch, aligned, packed),
@@ -932,7 +956,7 @@
             *[jax.ShapeDtypeStruct((1, ch), F32)] * 4,
         ),
         in_specs=[vmem] * 7 + [hbm] * 2,
-        out_specs=(vmem, vmem, hbm, hbm, vmem, vmem, vmem, vmem),
+        out_specs=(hbm, hbm, hbm, hbm, vmem, vmem, vmem, vmem),
         scratch_shapes=scratch,
         compiler_params=pltpu.CompilerParams(
             collective_id=0, has_side_effects=True, vmem_limit_bytes=60 * 1024 * 1024),

time: 117 us -> 117 us (level)
  no operation moved by 1% of the time
where the time goes in v1:
time: 117 us
  Pallas kernels  116 us (99%)
    pallas_call x1, Pallas kernels, per_device(): pl.pallas_call(functools.partial(block_kernel, n, s_count, rows, wide, ch...  112 us
    pallas_call x1, Pallas kernels, per_device(): pl.pallas_call(functools.partial(finish_kernel, 2 + len(moved)), out_shap...  3.75 us

profile of v1, /device:TPU:1, one launch (start us, length us, event | category | flops | bytes accessed | tf_op | source)
XLA Modules:
  0.0 117.0 jit_solution(16936696648815317809)
XLA Ops:
  0.6 112.4 %shard_map.152 = (bf16[64,2048]{1,0:T(8,128)(2,1)}, f32[64,2048]{1,0:T(8,128)}, bf16[2,4,144,512]{3,2,1,0:T(8,128)(2,1)}, bf16[2,4,144,512]{3,2,1,0:T(8,128)(2,1...) custom-call(bf16[64,2048]{1,0:T(8,128)(2,1)} %refs_0_.1, ...), custom_call_target="tpu_custom_call" | custom-call | tf_op jit(solution)/shard_map/pallas_call | solution.py:949
  113.1 3.7 %shard_map.153 = (f32[1152,512]{1,0:T(8,128)}, f32[1152,512]{1,0:T(8,128)}, bf16[64,2048]{1,0:T(8,128)(2,1)}, f32[64,2048]{1,0:T(8,128)}, f32[1,128]{1,0:T(1,128...) custom-call(bf16[1152,512]{1,0:T(8,128)(2,1)} %bitcast.17, bf16[1152,512]{1,0:T(8,128)(2,1)} %bitcast.18, ...), custom_call_target="tpu_custom_call" | custom-call | tf_op jit(solution)/shard_map/pallas_call | solution.py:975

commit v2 on v1

--- a/solution.py
+++ b/solution.py
@@ -15,7 +15,7 @@
 ROOT_HALF = 0.7071067811865476
 ROOT_TWO_PI = 0.3989422804014327
 CHUNK = 64
-FINISH_PARTS = 8
+FINISH_PARTS = 4
 UNROLL = 2
 HALVES = 2
 LARGE, SMALL = 7, 3
@@ -42,7 +42,7 @@
     (out_block, out_input, out_wg1, out_wg2, out_gain1, out_shift1, out_gain2, out_shift2) = refs[9:17]
     (turned, wv, wf, x_t, pack, unpack, places, edge_send, edge_recv, cot_send, cot_recv, cotm, mask, masked,
      normed1, normed2, through, slope1, hid, hid2, pad, acc, hold, taken,
-     part, psend, crecv, hsend, qrecv, wout, st_send, st_recv, row_send, row_recv, flat_block, flat_input,
+     part, psend, crecv, hsend, qrecv, wout, st_send, st_recv, row_send, row_recv, early, flat_block, flat_input,
      w_sem, wz_ssem, wz_rsem, wp_ssem, wp_rsem, e_ssem, e_rsem, ce_ssem, ce_rsem, ag_ssem, ag_rsem,
      st_ssem, st_rsem, row_ssem, row_rsem, c_ssem, c_rsem, q_ssem, q_rsem,
      f_ssem, f_rsem, h_ssem, h_rsem, o_sem, r_sem) = refs[17:]
@@ -217,10 +217,12 @@
             send_sem=row_ssem.at[slot, side], recv_sem=row_rsem.at[slot, 1 - side],
             device_id=(z, before if side == 0 else after), device_id_type=MESH)
 
-    def send_rows(slot, ref):
-        for side, start in ((0, 0), (1, cells - wide)):
-            row_send[slot, side] = ref[start:start + wide, :]
-            row_copy(slot, side).start()
+    def send_row(slot, side):
+        start = side * (cells - wide)
+        row_send[slot, side] = acc[start:start + wide, :]
+        row_copy(slot, side).start()
+
+    settled = (rows // HALVES - 1) * wide
 
     def take_rows(slot, ref):
         for side in range(2):
@@ -385,6 +387,8 @@
                     consume_way(k, q, (near + i) % 2, consume)
             each(k)
 
+    last_step = jnp.maximum(z, n - 1 - z)
+
     last_pass = jnp.maximum(jnp.where(z < n - 1, z, 0), jnp.where(z > 0, n - 1 - z, 0))
 
     def forward(ph, field):
@@ -402,6 +406,9 @@
                 if q == 0:
                     weights_arrived(ph, slot)
                 add_conv(q, into, lambda a: wf[ph, slot, 3 * a * ch:3 * (a + 1) * ch, :])
+
+            if q == 0:
+                pl.when(k == last_step)(lambda: early_moments(ph))
 
         def each(k):
             if ph == 0:
@@ -570,6 +577,20 @@
         field_grad(ph, block)
         sum_cores(ph, block)
 
+    def inner_sums(first, last, side):
+        start = side * (cells - wide)
+        row_send[2, side] = acc[start:start + wide, :]
+        at = slice(first, last)
+        v = acc[at, :] * slope1[at, :]
+        slope1[at, :] = v
+        acc[at, :] = jnp.zeros((last - first, ch), F32)
+        return fold(v * normed1[at, :]), fold(v)
+
+    def early_inner():
+        for i, v in enumerate(inner_sums(0, settled, 0)):
+            early[8 * i:8 * i + 8, :] = v
+        row_copy(2, 0).start()
+
     def backward(ph):
         last = ph == 0
 
@@ -581,6 +602,8 @@
                 def _():
                     make_grad(ph, block)
             add_conv(q, into, None, lambda t: wv[ph, block, t * ch:(t + 1) * ch, :])
+            if q == 0 and not last:
+                pl.when(k == last_step)(early_inner)
 
         def each(k):
             first, end = made_at(k)
@@ -607,31 +630,38 @@
 
     zero = jnp.zeros((8, ch), F32)
 
-    def local_moments(ref):
-        def sums(start, size, carry):
-            at = pl.ds(start, size)
-            m = mask[at, :]
-            return carry[0] + fold(ref[at, :] * m), carry[1] + fold(m)
-        added, number = (flatten(v) for v in chunked(sums, (zero, zero)))
-        middle = added / jnp.maximum(number, 1.0)
-
-        def spread(start, size, carry):
-            at = pl.ds(start, size)
-            c = (ref[at, :] - middle) * mask[at, :]
-            return carry + fold(c * c)
-        return added, number, flatten(chunked(spread, zero))
+    def part_moments(first, last):
+        m = mask[first:last, :]
+        v = acc[first:last, :]
+        number, added = flatten(fold(m)), flatten(fold(v * m))
+        c = (v - added / jnp.maximum(number, 1.0)) * m
+        return added, number, flatten(fold(c * c))
+
+    def early_moments(slot):
+        for i, v in enumerate(part_moments(0, settled)):
+            early[i:i + 1, :] = v
+        send_row(slot, 0)
+
+    def combine(added, number, spread):
+        total_added, total_number = sum(added), sum(number)
+        mean = total_added / jnp.maximum(total_number, 1.0)
+        about = 0.0
+        for a, k, q in zip(added, number, spread):
+            off = a / jnp.maximum(k, 1.0) - mean
+            about = about + (q + k * off * off)
+        return total_added, total_number, about
+
+    def local_moments():
+        late = part_moments(settled, cells)
+        return combine(*([early[i:i + 1, :], v] for i, v in enumerate(late)))
 
     def moments(slot):
         take_stats(slot)
-        got = [st_recv[slot, k] for k in range(s_count)]
-        added = sum(g[0:1] for g in got)
-        number = sum(g[1:2] for g in got)
-        mean = added / number
-        spread = 0.0
-        for g in got:
-            off = g[0:1] / jnp.maximum(g[1:2], 1.0) - mean
-            spread = spread + (g[2:3] + g[1:2] * off * off)
-        return mean, lax.rsqrt(spread / number + EPSILON), number
+        added, number, about = (st_recv[slot, :, i, :] for i in range(3))
+        count = flatten(number)
+        mean = flatten(added) / count
+        off = added / jnp.maximum(number, 1.0) - mean
+        return mean, lax.rsqrt(flatten(about + number * off * off) / count + EPSILON), count
 
     def everywhere(fn):
         chunked(fn, 0)
@@ -722,8 +752,8 @@
     for h in range(HALVES):
         make_unpack(h)
     forward(0, masked)
-    send_rows(0, acc)
-    send_stats(0, local_moments(acc))
+    send_stats(0, local_moments())
+    send_row(0, 1)
     weights_round(1)
     mean1, scale1, count = moments(0)
 
@@ -746,8 +776,8 @@
     pack_field(1, hid, activate_one)
     everywhere(slope_one)
     forward(1, hid)
-    send_rows(1, acc)
-    send_stats(1, local_moments(acc))
+    send_stats(1, local_moments())
+    send_row(1, 1)
     turn_field(0, masked)
     turn_field(1, hid)
     weights_sent(0)
@@ -786,8 +816,7 @@
 
     def gradient_sums(slot):
         take_stats(slot)
-        got = [st_recv[slot, k] for k in range(s_count)]
-        return sum(g[0:1] for g in got), sum(g[1:2] for g in got)
+        return flatten(st_recv[slot, :, 0, :]), flatten(st_recv[slot, :, 1, :])
 
     def norm_back(upstream, normed, gain, scale, sums):
         gain_grad, shift_grad = sums
@@ -805,16 +834,9 @@
     pack_field(3, hid, norm_back(through, normed2, gain2, scale2, sums2))
     backward(1)
 
-    send_rows(2, acc)
-
-    def inner_main(start, size, carry):
-        at = pl.ds(start, size)
-        v = acc[at, :] * slope1[at, :]
-        slope1[at, :] = v
-        acc[at, :] = jnp.zeros((size, ch), F32)
-        return carry[0] + fold(v * normed1[at, :]), carry[1] + fold(v)
-
-    send_stats(3, [flatten(v) for v in chunked(inner_main, (zero, zero))])
+    parts = inner_sums(settled, cells, 1)
+    send_stats(3, [flatten(early[8 * i:8 * i + 8, :] + v) for i, v in enumerate(parts)])
+    row_copy(2, 1).start()
 
     @pl.when(jnp.logical_not(passing))
     def _():
@@ -929,6 +951,7 @@
         pltpu.VMEM((4, s_count, 8, ch), F32),
         pltpu.VMEM((3, 2, wide, ch), F32),
         pltpu.VMEM((3, 2, wide, ch), F32),
+        pltpu.VMEM((16, ch), F32),
         pltpu.VMEM((rows, ch * wide), BF16),
         pltpu.VMEM((rows, ch * wide), F32),
         sem((2, n)),

time: 117 us -> 117 us (level)
  no operation moved by 1% of the time
where the time goes in v2:
time: 117 us
  Pallas kernels  116 us (99%)
    pallas_call x1, Pallas kernels, per_device(): pl.pallas_call(functools.partial(block_kernel, n, s_count, rows, wide, ch...  112 us
    pallas_call x1, Pallas kernels, per_device(): pl.pallas_call(functools.partial(finish_kernel, 2 + len(moved)), out_shap...  3.68 us

profile of v2, /device:TPU:1, one launch (start us, length us, event | category | flops | bytes accessed | tf_op | source)
XLA Modules:
  0.0 116.8 jit_solution(980220381456217675)
XLA Ops:
  0.6 112.3 %shard_map.152 = (bf16[64,2048]{1,0:T(8,128)(2,1)}, f32[64,2048]{1,0:T(8,128)}, bf16[2,4,144,512]{3,2,1,0:T(8,128)(2,1)}, bf16[2,4,144,512]{3,2,1,0:T(8,128)(2,1...) custom-call(bf16[64,2048]{1,0:T(8,128)(2,1)} %refs_0_.1, ...), custom_call_target="tpu_custom_call" | custom-call | tf_op jit(solution)/shard_map/pallas_call | solution.py:972
  112.9 3.7 %shard_map.153 = (f32[1152,512]{1,0:T(8,128)}, f32[1152,512]{1,0:T(8,128)}, bf16[64,2048]{1,0:T(8,128)(2,1)}, f32[64,2048]{1,0:T(8,128)}, f32[1,128]{1,0:T(1,128...) custom-call(bf16[1152,512]{1,0:T(8,128)(2,1)} %bitcast.17, bf16[1152,512]{1,0:T(8,128)(2,1)} %bitcast.18, ...), custom_call_target="tpu_custom_call" | custom-call | tf_op jit(solution)/shard_map/pallas_call | solution.py:998

commit v3 on v2

--- a/solution.py
+++ b/solution.py
@@ -43,7 +43,7 @@
     (turned, wv, wf, x_t, pack, unpack, places, edge_send, edge_recv, cot_send, cot_recv, cotm, mask, masked,
      normed1, normed2, through, slope1, hid, hid2, pad, acc, hold, taken,
      part, psend, crecv, hsend, qrecv, wout, st_send, st_recv, row_send, row_recv, early, flat_block, flat_input,
-     w_sem, wz_ssem, wz_rsem, wp_ssem, wp_rsem, e_ssem, e_rsem, ce_ssem, ce_rsem, ag_ssem, ag_rsem,
+     w_sem, wz_ssem, wz_rsem, wp_ssem, wp_rsem, wh_ssem, wh_rsem, e_ssem, e_rsem, ce_ssem, ce_rsem, ag_ssem, ag_rsem,
      st_ssem, st_rsem, row_ssem, row_rsem, c_ssem, c_rsem, q_ssem, q_rsem,
      f_ssem, f_rsem, h_ssem, h_rsem, o_sem, r_sem) = refs[17:]
 
@@ -55,6 +55,9 @@
     core, chip, chips = s % 2, s // 2, s_count // 2
     before, after = (s + s_count - 1) % s_count, (s + 1) % s_count
     tap_rows = 9 * ch
+    half_rows = tap_rows // 2
+    owners = math.gcd(half_rows // 16, chips)
+    piece = half_rows // owners
 
     barrier = pltpu.get_barrier_semaphore()
 
@@ -165,8 +168,11 @@
     w_mine = s % w_parts
     w_group = s - w_mine
 
+    c_group = chip - chip % owners
+    c_mine = core * half_rows + (chip % owners) * piece
+
     def wz_copy(which, k):
-        at = pl.ds(w_mine * w_rows, w_rows)
+        at = pl.ds(c_mine, piece) if which else pl.ds(w_mine * w_rows, w_rows)
         slot = n - k - 1
         return pltpu.make_async_remote_copy(
             src_ref=wv.at[which, (z + k) % n, at, :], dst_ref=wf.at[which, slot, at, :],
@@ -174,11 +180,29 @@
             device_id=((z + k) % n, s), device_id_type=MESH)
 
     def wp_copy(which, slot, k, whose):
-        at = pl.ds(whose * w_rows, w_rows)
+        if which:
+            at = pl.ds(core * half_rows + whose * piece, piece)
+            to = (c_group + (chip + k) % owners) * 2 + core
+        else:
+            at = pl.ds(whose * w_rows, w_rows)
+            to = w_group + (w_mine + k) % w_parts
         return pltpu.make_async_remote_copy(
             src_ref=wf.at[which, slot, at, :], dst_ref=wf.at[which, slot, at, :],
             send_sem=wp_ssem.at[which, slot, k], recv_sem=wp_rsem.at[which, slot, whose],
-            device_id=(z, w_group + (w_mine + k) % w_parts), device_id_type=MESH)
+            device_id=(z, to), device_id_type=MESH)
+
+    def wh_copy(slot, whose):
+        at = pl.ds(whose * half_rows, half_rows)
+        return pltpu.make_async_remote_copy(
+            src_ref=wf.at[1, slot, at, :], dst_ref=wf.at[1, slot, at, :],
+            send_sem=wh_ssem.at[slot], recv_sem=wh_rsem.at[slot],
+            device_id=(z, chip * 2 + 1 - core), device_id_type=MESH)
+
+    def weights_to_core():
+        for slot in range(n - 1):
+            for k in range(1, owners):
+                wp_copy(1, slot, k, (chip + k) % owners).wait_recv()
+            wh_copy(slot, core).start()
 
     def weights_over_z(which):
         for copy in w_copies[which * n:(which + 1) * n]:
@@ -202,14 +226,17 @@
                     slot = slot_of(block)
                     wz_copy(which, n - 1 - slot).wait_recv()
 
-                    @pl.loop(1, w_parts)
+                    @pl.loop(1, owners if which else w_parts)
                     def _(k):
-                        wp_copy(which, slot, k, w_mine).start()
+                        wp_copy(which, slot, k, chip % owners if which else w_mine).start()
 
     def weights_arrived(which, slot):
-        @pl.loop(1, w_parts)
-        def _(k):
-            wp_copy(which, slot, k, (w_mine + k) % w_parts).wait_recv()
+        if which:
+            wh_copy(slot, 1 - core).wait_recv()
+        else:
+            @pl.loop(1, w_parts)
+            def _(k):
+                wp_copy(which, slot, k, (w_mine + k) % w_parts).wait_recv()
 
     def row_copy(slot, side):
         return pltpu.make_async_remote_copy(
@@ -411,7 +438,9 @@
                 pl.when(k == last_step)(lambda: early_moments(ph))
 
         def each(k):
-            if ph == 0:
+            if ph == 1:
+                pl.when(k == 0)(weights_to_core)
+            else:
                 @pl.when(k == 0)
                 def _():
                     weights_round(0)
@@ -439,9 +468,6 @@
             for a, v in enumerate((left, here, right)):
                 x_t[ph, a * ch:(a + 1) * ch, i * ch:(i + 1) * ch] = v.astype(BF16)
 
-    half_rows = tap_rows // 2
-    owners = math.gcd(half_rows // 16, chips)
-    piece = half_rows // owners
 
     def c_copy(ph, j):
         return pltpu.make_async_remote_copy(
@@ -724,10 +750,13 @@
         for k in range(1, n):
             wz_copy(which, k).wait_send()
 
-        @pl.loop(1, w_parts)
+        @pl.loop(1, owners if which else w_parts)
         def _(k):
             for slot in range(n - 1):
-                wp_copy(which, slot, k, w_mine).wait_send()
+                wp_copy(which, slot, k, chip % owners if which else w_mine).wait_send()
+        if which:
+            for slot in range(n - 1):
+                wh_copy(slot, core).wait_send()
 
     def grads_sent(ph):
         @pl.loop(0, n)
@@ -957,6 +986,7 @@
         sem((2, n)),
         sem((2, n)), sem((2, n)),
         sem((2, n - 1, s_count)), sem((2, n - 1, s_count)),
+        sem((n - 1,)), sem((n - 1,)),
         sem((2,)), sem((2,)),
         sem((2,)), sem((2,)),
         sem((4, 2, n, HALVES)), sem((4, n, HALVES)),

time: 117 us -> 117 us (level)
  no operation moved by 1% of the time
where the time goes in v3:
time: 117 us
  Pallas kernels  116 us (99%)
    pallas_call x1, Pallas kernels, per_device(): pl.pallas_call(functools.partial(block_kernel, n, s_count, rows, wide, ch...  112 us
    pallas_call x1, Pallas kernels, per_device(): pl.pallas_call(functools.partial(finish_kernel, 2 + len(moved)), out_shap...  3.68 us

profile of v3, /device:TPU:1, one launch (start us, length us, event | category | flops | bytes accessed | tf_op | source)
XLA Modules:
  0.0 116.8 jit_solution(9046945676268039559)
XLA Ops:
  0.6 112.3 %shard_map.152 = (bf16[64,2048]{1,0:T(8,128)(2,1)}, f32[64,2048]{1,0:T(8,128)}, bf16[2,4,144,512]{3,2,1,0:T(8,128)(2,1)}, bf16[2,4,144,512]{3,2,1,0:T(8,128)(2,1...) custom-call(bf16[64,2048]{1,0:T(8,128)(2,1)} %refs_0_.1, ...), custom_call_target="tpu_custom_call" | custom-call | tf_op jit(solution)/shard_map/pallas_call | solution.py:1002
  113.0 3.7 %shard_map.153 = (f32[1152,512]{1,0:T(8,128)}, f32[1152,512]{1,0:T(8,128)}, bf16[64,2048]{1,0:T(8,128)(2,1)}, f32[64,2048]{1,0:T(8,128)}, f32[1,128]{1,0:T(1,128...) custom-call(bf16[1152,512]{1,0:T(8,128)(2,1)} %bitcast.17, bf16[1152,512]{1,0:T(8,128)(2,1)} %bitcast.18, ...), custom_call_target="tpu_custom_call" | custom-call | tf_op jit(solution)/shard_map/pallas_call | solution.py:1028

commit v4 on v2

--- a/solution.py
+++ b/solution.py
@@ -423,6 +423,8 @@
                 @pl.when(k == last_pass)
                 def _():
                     load_cotangent()
+            if ph == 1:
+                pl.when(k == last_pass)(lambda: everywhere(slope_one))
         (gather if ph else gather_passing_first)(ph, consume, each)
 
     def turn_field(ph, field):
@@ -774,7 +776,6 @@
 
     take_rows(0, normed1)
     pack_field(1, hid, activate_one)
-    everywhere(slope_one)
     forward(1, hid)
     send_stats(1, local_moments())
     send_row(1, 1)

time: 117 us -> 117 us (level)
  no operation moved by 1% of the time
where the time goes in v4:
time: 117 us
  Pallas kernels  116 us (99%)
    pallas_call x1, Pallas kernels, per_device(): pl.pallas_call(functools.partial(block_kernel, n, s_count, rows, wide, ch...  112 us
    pallas_call x1, Pallas kernels, per_device(): pl.pallas_call(functools.partial(finish_kernel, 2 + len(moved)), out_shap...  3.68 us

profile of v4, /device:TPU:1, one launch (start us, length us, event | category | flops | bytes accessed | tf_op | source)
XLA Modules:
  0.0 116.8 jit_solution(17178327700371722327)
XLA Ops:
  0.6 112.3 %shard_map.152 = (bf16[64,2048]{1,0:T(8,128)(2,1)}, f32[64,2048]{1,0:T(8,128)}, bf16[2,4,144,512]{3,2,1,0:T(8,128)(2,1)}, bf16[2,4,144,512]{3,2,1,0:T(8,128)(2,1...) custom-call(bf16[64,2048]{1,0:T(8,128)(2,1)} %refs_0_.1, ...), custom_call_target="tpu_custom_call" | custom-call | tf_op jit(solution)/shard_map/pallas_call | solution.py:973
  112.9 3.7 %shard_map.153 = (f32[1152,512]{1,0:T(8,128)}, f32[1152,512]{1,0:T(8,128)}, bf16[64,2048]{1,0:T(8,128)(2,1)}, f32[64,2048]{1,0:T(8,128)}, f32[1,128]{1,0:T(1,128...) custom-call(bf16[1152,512]{1,0:T(8,128)(2,1)} %bitcast.17, bf16[1152,512]{1,0:T(8,128)(2,1)} %bitcast.18, ...), custom_call_target="tpu_custom_call" | custom-call | tf_op jit(solution)/shard_map/pallas_call | solution.py:999
